TPU v7x, 512 devices: a whole 4x8x8 slice. The times are simulated.
512 devices in a mesh: grp: 16 (over z, y_hi), seq: 32 (over x, y_lo, core).
Axes of the slice: x: 4, y: 8 (y_hi: 2, y_lo: 4; y = y_hi * 4 + y_lo), z: 8, core: 2. Of those that a mesh axis runs over, the one named last changes fastest.
Arguments:
- hidden: bfloat16 [512, 4096], P('seq'), may hold values from -1.5 to 1.5
- norm_gain: float32 [4096], replicated, may hold values from 0.25 to 1.75
- w_query: bfloat16 [4096, 2048], P('seq', 'grp'), may hold values from -0.09375 to 0.09375
- w_out: bfloat16 [2048, 4096], P('grp', 'seq'), may hold values from -0.125 to 0.125
- enc_cache: bfloat16 [2, 262144, 2048], P(None, 'seq', 'grp')
- lengths: int32 [512], replicated, may hold values from 1 to 262144, as said below
Outputs:
- mixed: bfloat16 [512, 4096], P('seq', 'grp')
Inputs may be any that keep to these rules, and one draw needn't show every extreme that they name: `lengths`: every row has at least one valid position; some row in each draw has all 262144 positions valid.
All inputs are finite; a program needn't handle non-finite values.
Results may differ from a plain program's by a relative error of at most 0.02.
The roundings to bfloat16 on the way count: a program that leaves them out, or rounds other values in their place, can miss the bound.
Values may be sent and summed in bfloat16 or wider, within the bound.
A program may use at most 64 MiB of HBM per device.

v0:
```python
import jax
import jax.numpy as jnp
from jax import lax
from jax.sharding import PartitionSpec as P

HEAD_DIM = 64


def combined_all(value, axis, join):
    pieces = jax.tree.map(lambda part: lax.all_gather(part, axis), value)
    head = jax.tree.map(lambda part: part[0], pieces)
    tail = jax.tree.map(lambda part: part[1:], pieces)
    total, _ = lax.scan(lambda total, slab: (join(total, slab), None), head, tail)
    return total


def combine_parts(earlier, later):
    peak = jnp.maximum(earlier[0], later[0])
    factor_one = jnp.exp(earlier[0] - peak)
    factor_two = jnp.exp(later[0] - peak)
    total = earlier[1] * factor_one + later[1] * factor_two
    accum = earlier[2] * factor_one[..., None] + later[2] * factor_two[..., None]
    return (peak, total, accum)


def attend(queries, enc_keys, enc_values, lengths, offset):
    rows_all = queries.shape[0]
    local_heads = queries.shape[1]
    head_size = queries.shape[2]
    row_block = min(128, rows_all)
    key_block = min(1024, enc_keys.shape[0])
    row_count = rows_all // row_block
    key_count = enc_keys.shape[0] // key_block
    query_blocks = queries.reshape(row_count, row_block, local_heads, head_size)
    length_blocks = lengths.reshape(row_count, row_block)
    key_blocks = enc_keys.reshape(key_count, key_block, local_heads, head_size)
    value_blocks = enc_values.reshape(key_count, key_block, local_heads, head_size)
    block_starts = jnp.arange(key_count, dtype=jnp.int32) * key_block

    def rows_step(inputs):
        query_rows, row_lengths = inputs

        def key_step(state_now, pieces):
            key_rows, value_rows, block_first = pieces
            peak, total, accum = state_now
            positions = offset + block_first + jnp.arange(key_block, dtype=jnp.int32)
            valid = (positions[None, :] < row_lengths[:, None])[None]
            score = jnp.einsum(
                "rhd,khd->hrk", query_rows, key_rows, preferred_element_type=jnp.float32
            )
            masked = jnp.where(valid, score, jnp.float32(-1e30))
            new_peak = jnp.maximum(peak, jnp.max(masked, axis=-1))
            weights = jnp.where(valid, jnp.exp(score - new_peak[..., None]), jnp.float32(0.0))
            factor = jnp.exp(peak - new_peak)
            new_total = total * factor + jnp.sum(weights, axis=-1)
            product = jnp.einsum(
                "hrk,khd->hrd",
                weights.astype(jnp.bfloat16),
                value_rows,
                preferred_element_type=jnp.float32,
            )
            result = (new_peak, new_total, accum * factor[..., None] + product)
            return (result, None)

        start_state = (
            jnp.full((local_heads, row_block), -1e30, jnp.float32),
            jnp.zeros((local_heads, row_block), jnp.float32),
            jnp.zeros((local_heads, row_block, head_size), jnp.float32),
        )
        final_state, unused = lax.scan(
            key_step, start_state, (key_blocks, value_blocks, block_starts)
        )
        return final_state

    peaks, totals, accums = lax.map(rows_step, (query_blocks, length_blocks))
    peaks = peaks.transpose(1, 0, 2).reshape(local_heads, rows_all)
    totals = totals.transpose(1, 0, 2).reshape(local_heads, rows_all)
    accums = accums.transpose(1, 0, 2, 3).reshape(local_heads, rows_all, head_size)
    return (peaks, totals, accums)


def body(hidden, norm_gain, w_query, w_out, enc_cache, lengths):
    own_rows = hidden.shape[0]
    local_width = w_query.shape[1]
    head_size = HEAD_DIM
    local_heads = local_width // head_size
    wide = hidden.astype(jnp.float32)
    scale = lax.rsqrt(jnp.mean(wide * wide, axis=-1, keepdims=True) + 1e-06)
    normed = (wide * scale * norm_gain).astype(jnp.bfloat16)
    own_queries = jnp.dot(
        normed,
        lax.all_gather(w_query, "seq", axis=0, tiled=True),
        preferred_element_type=jnp.float32,
    ).astype(jnp.bfloat16)
    queries = lax.all_gather(own_queries, "seq", axis=0, tiled=True)
    rows_all = queries.shape[0]
    enc_local = enc_cache.shape[1]
    offset = lax.axis_index("seq") * enc_local
    query_heads = queries.reshape(rows_all, local_heads, head_size)
    enc_keys = enc_cache[0].reshape(enc_local, local_heads, head_size)
    enc_values = enc_cache[1].reshape(enc_local, local_heads, head_size)
    peaks, totals, accums = attend(query_heads, enc_keys, enc_values, lengths, offset)
    row_first = lax.axis_index("seq") * own_rows
    peak_all, total_all, accum_all = combined_all((peaks, totals, accums), "seq", combine_parts)
    own_total = lax.dynamic_slice_in_dim(total_all, row_first, own_rows, 1)
    own_accum = lax.dynamic_slice_in_dim(accum_all, row_first, own_rows, 1)
    attended = (
        (own_accum / own_total[..., None])
        .transpose(1, 0, 2)
        .reshape(own_rows, local_width)
        .astype(jnp.bfloat16)
    )
    terms = jnp.dot(
        attended,
        lax.all_gather(w_out, "seq", axis=1, tiled=True),
        preferred_element_type=jnp.float32,
    )
    summed = lax.psum_scatter(
        terms.astype(jnp.bfloat16), "grp", scatter_dimension=1, tiled=True
    ).astype(jnp.float32)
    col_width = summed.shape[1]
    residual = lax.dynamic_slice_in_dim(wide, lax.axis_index("grp") * col_width, col_width, 1)
    return (residual + summed).astype(jnp.bfloat16)


def solution(mesh):
    placed = (P("seq", None), P(), P("seq", "grp"), P("grp", "seq"), P(None, "seq", "grp"), P())
    return jax.shard_map(
        body, mesh=mesh, in_specs=placed, out_specs=P("seq", "grp"), check_vma=False
    )
```

profile of v0, /device:TPU:1, one launch (start us, length us, event | category | flops | bytes accessed | tf_op | source)
XLA Modules:
  0.0 556.2 jit_solution(6842958449589432790)
XLA Ops:
  7.3 3.8 fusion.26
  11.2 3.3 reshape.51
  14.4 9.1 %copy.25 = bf16[8,1024,2,64]{1,3,2,0:T(8,128)(2,1)S(1)} copy(bf16[8,1024,2,64]{3,2,1,0:T(2,128)(2,1)} %reshape.51) | data formatting | bytes 4194304
  23.5 8.2 %reshape.52 = bf16[8,1024,2,64]{3,2,1,0:T(2,128)(2,1)} reshape(bf16[1,8192,128]{2,1,0:T(8,128)(2,1)} %get-tuple-element.325) | data formatting | bytes 4194304 | tf_op jit(solution)/shard_map/reshape;reshape;squeeze | solution.py:37
  31.7 10.7 %copy.26 = bf16[8,1024,2,64]{1,3,2,0:T(8,128)(2,1)} copy(bf16[8,1024,2,64]{3,2,1,0:T(2,128)(2,1)} %reshape.52) | data formatting | bytes 4194304
  42.6 34.3 %all-gather.4.cloned.1.call-done = bf16[4096,128]{1,0:T(8,128)(2,1)} async-done(((bf16[128,128]{1,0:T(8,128)(2,1)}), bf16[4096,128]{1,0:T(8,128)(2,1)}) %all-gather.4.cloned.1.call-update) | async-done | bytes 1048592 | tf_op jit(solution)/shard_map/all_gather | solution.py:92
  76.9 1.5 convolution_convert_fusion.1
  78.4 41.2 %all_gather.19 = bf16[512,128]{1,0:T(8,128)(2,1)S(1)} all-gather(bf16[16,128]{1,0:T(8,128)(2,1)S(1)} %convolution_convert_fusion.1), channel_id=1, replica_groups=mesh['grp'=16,'seq'=32] {'seq'}, dimensions={0}, use_global_device_ids=true | all-gather | bytes 135168 | tf_op jit(solution)/shard_map/all_gather | solution.py:95
  120.5 119.5 %while.47 = (s32[]{:T(128)}, f32[4,2,128]{2,1,0:T(2,128)S(1)}, f32[4,2,128]{2,1,0:T(2,128)S(1)}, f32[4,2,128,64]{2,3,1,0:T(8,128)}, s32[4,128]{1,0:T(4,128)}, /*...) while((s32[]{:T(128)}, f32[4,2,128]{2,1,0:T(2,128)S(1)}, ...), condition=%wide.region_6.7_spmd.clone, body=%wide.region_1.6_spmd.clone.sunk | while | flops 69388552 | bytes 4586418 | solution.py:75
  121.9 27.7 %while.48 = (s32[]{:T(128)}, f32[2,128]{1,0:T(2,128)S(1)}, f32[2,128]{1,0:T(2,128)S(1)}, f32[2,128,64]{1,2,0:T(8,128)S(1)}, s32[8]{0:T(128)S(1)}, /*index=5*/s32...) while((s32[]{:T(128)}, f32[2,128]{1,0:T(2,128)S(1)}, ...), condition=%wide.region_5.5_spmd.clone, body=%wide.region_2.4_spmd.clone.sunk | while | flops 69388544 | bytes 4383905 | solution.py:70
  127.5 1.3 convolution_add_fusion.2
  131.0 1.3 convolution_add_fusion.2
  134.4 1.3 convolution_add_fusion.2
  137.9 1.3 convolution_add_fusion.2
  141.4 1.3 convolution_add_fusion.2
  144.8 1.3 convolution_add_fusion.2
  148.3 1.3 convolution_add_fusion.2
  151.8 27.7 %while.48 = (s32[]{:T(128)}, f32[2,128]{1,0:T(2,128)S(1)}, f32[2,128]{1,0:T(2,128)S(1)}, f32[2,128,64]{1,2,0:T(8,128)S(1)}, s32[8]{0:T(128)S(1)}, /*index=5*/s32...) while((s32[]{:T(128)}, f32[2,128]{1,0:T(2,128)S(1)}, ...), condition=%wide.region_5.5_spmd.clone, body=%wide.region_2.4_spmd.clone.sunk | while | flops 69388544 | bytes 4383905 | solution.py:70
  157.4 1.3 convolution_add_fusion.2
  160.8 1.3 convolution_add_fusion.2
  171.2 1.3 convolution_add_fusion.2
  174.7 1.3 convolution_add_fusion.2
  178.2 1.3 convolution_add_fusion.2
  181.6 27.8 %while.48 = (s32[]{:T(128)}, f32[2,128]{1,0:T(2,128)S(1)}, f32[2,128]{1,0:T(2,128)S(1)}, f32[2,128,64]{1,2,0:T(8,128)S(1)}, s32[8]{0:T(128)S(1)}, /*index=5*/s32...) while((s32[]{:T(128)}, f32[2,128]{1,0:T(2,128)S(1)}, ...), condition=%wide.region_5.5_spmd.clone, body=%wide.region_2.4_spmd.clone.sunk | while | flops 69388544 | bytes 4383905 | solution.py:70
  190.7 1.3 convolution_add_fusion.2
  211.5 27.8 %while.48 = (s32[]{:T(128)}, f32[2,128]{1,0:T(2,128)S(1)}, f32[2,128]{1,0:T(2,128)S(1)}, f32[2,128,64]{1,2,0:T(8,128)S(1)}, s32[8]{0:T(128)S(1)}, /*index=5*/s32...) while((s32[]{:T(128)}, f32[2,128]{1,0:T(2,128)S(1)}, ...), condition=%wide.region_5.5_spmd.clone, body=%wide.region_2.4_spmd.clone.sunk | while | flops 69388544 | bytes 4383905 | solution.py:70
  242.7 38.9 %all_gather.21 = f32[32,2,512]{2,1,0:T(2,128)S(1)} all-gather(f32[1,2,512]{2,1,0:T(2,128)S(1)} %bitcast.80), channel_id=1, replica_groups=mesh['grp'=16,'seq'=32] {'seq'}, dimensions={0}, use_global_device_ids=true | all-gather | bytes 135168 | tf_op jit(solution)/shard_map/all_gather | solution.py:10
  281.6 40.2 %all_gather.20 = f32[32,2,512]{2,1,0:T(2,128)S(1)} all-gather(f32[1,2,512]{2,1,0:T(2,128)S(1)} %bitcast.79), channel_id=1, replica_groups=mesh['grp'=16,'seq'=32] {'seq'}, dimensions={0}, use_global_device_ids=true | all-gather | bytes 135168 | tf_op jit(solution)/shard_map/all_gather | solution.py:10
  323.1 8.2 %slice.37 = f32[31,2,512,64]{2,3,1,0:T(8,128)} slice(f32[32,2,512,64]{2,3,1,0:T(8,128)} %all-gather.6.cloned.1.call-done), slice={[1:32], [0:2], [0:512], [0:64]} | slice | bytes 16252928 | tf_op jit(solution)/shard_map/slice | solution.py:12
  331.2 52.5 %while.45 = (s32[]{:T(128)}, f32[2,512]{1,0:T(2,128)S(1)}, f32[2,512]{1,0:T(2,128)S(1)}, f32[2,512,64]{2,1,0:T(8,128)S(1)}, f32[31,2,512]{2,1,0:T(2,128)S(1)}, /...) while((s32[]{:T(128)}, f32[2,512]{1,0:T(2,128)S(1)}, f32[2,512]{1,0:T(2,128)S(1)}, ...), condition=%wide.region_8.9_spmd, body=%wide.region_7.8_spmd.sunk | while | flops 202754 | bytes 1876061 | solution.py:13
  384.0 2.1 convolution_convert_fusion
  386.2 162.1 %reduce-scatter.2.cloned.1.call-done = bf16[16,256]{1,0:T(8,128)(2,1)} async-done(((bf16[16,4096]{1,0:T(8,128)(2,1)}), bf16[16,256]{1,0:T(8,128)(2,1)}) %reduce-scatter.2.cloned.1.call-update) | async-done | bytes 8208 | tf_op jit(solution)/shard_map/reduce_scatter | solution.py:118
  (466 shorter events, 138.8 us)
Async XLA Ops:
  6.5 70.3 %all-gather.4.cloned.1.call-start = ((), (), s32[]{:S(2)}) async-start(), calls=%async_computation.1 | async-start | bytes 1081344 | tf_op jit(solution)/shard_map/all_gather | solution.py:92
  7.3 314.6 %all-gather.6.cloned.1.call-start = ((), (), s32[]{:S(2)}) async-start(), calls=%async_computation.2 | async-start | bytes 8650752 | tf_op jit(solution)/shard_map/all_gather | solution.py:10
  31.7 10.7 %copy-start = (bf16[16,4096]{1,0:T(8,128)(2,1)S(1)}, bf16[16,4096]{1,0:T(8,128)(2,1)}, u32[]{:S(2)}) copy-start(bf16[16,4096]{1,0:T(8,128)(2,1)} %param.12) | copy-start | bytes 393220
  31.7 45.1 %copy-start.1 = (f32[4096]{0:T(1024)S(1)}, f32[4096]{0:T(1024)}, u32[]{:S(2)}) copy-start(f32[4096]{0:T(1024)} %param.13) | copy-start | bytes 49156
  241.9 142.1 %all-gather.8.cloned.1.call-start = ((), (), s32[]{:S(2)}) async-start(), calls=%async_computation.3 | async-start | bytes 1081344 | tf_op jit(solution)/shard_map/all_gather | solution.py:115
  242.7 305.7 %reduce-scatter.2.cloned.1.call-start = ((), (), s32[]{:S(2)}) async-start(), calls=%async_computation.4 | async-start | bytes 139264 | tf_op jit(solution)/shard_map/reduce_scatter | solution.py:118
Sparse Core Ops, SparseCore 0:
  9.5 67.3 all-gather.3
  242.1 69.9 all-gather.5
  314.2 61.8 all-gather.7
  386.3 162.0 reduce-scatter.1
where the time goes:
time: 564 us; the launch traced here: 556 us
  waiting for transfers between devices  198 us (35%)
  blocking collectives  120 us (21%)
  local copies, waits for them, and re-layouts  112 us (20%)
  matrix products  58.4 us (10%)
  other arithmetic  31.4 us (6%)
  loops' own time  23.2 us (4%)
  between operations  13.3 us (2%)
    reduce_scatter x1, waiting for transfers between devices, body(): lax.psum_scatter(terms.astype(jnp.bfloat16), 'grp', scatter_dimension=1,...  162 us
    all_gather x2, blocking collectives, combined_all(): pieces = jax.tree.map(lambda part: lax.all_gather(part, axis), value)  79.1 us
    dot_general x32, matrix products, key_step(): jnp.einsum('hrk,khd->hrd', weights.astype(jnp.bfloat16), value_rows, pref...  42.8 us
    all_gather x1, blocking collectives, body(): queries = lax.all_gather(own_queries, 'seq', axis=0, tiled=True)  41.2 us
    dynamic_slice x62, local copies, waits for them, and re-layouts, combined_all(): lax.scan(lambda total, slab: (join(total, slab), None), head, tail)  36.3 us
    all_gather x1, waiting for transfers between devices, body(): lax.all_gather(w_query, 'seq', axis=0, tiled=True)  34.3 us
    another operation x4, loops' own time, rows_step(): lax.scan(key_step, start_state, (key_blocks, value_blocks, block_starts))  22.2 us
    unnamed x7, local copies, waits for them, and re-layouts  20.6 us
  transfers between devices with their start and end apart: 4, of which 2 were waited for; matrix products, arithmetic and copies ran while one was open for 17% of the time, Pallas kernels for 0%

commit v1 on v0

v1 whole, which is shorter than its diff:
```python
import jax
import jax.numpy as jnp
from jax import lax
from jax.experimental import pallas as pl
from jax.experimental.pallas import tpu as pltpu
from jax.sharding import PartitionSpec as P

MESH = pl.DeviceIdType.MESH
F32 = jnp.float32
BF16 = jnp.bfloat16
NT = (((1,), (1,)), ((), ()))
LOG2E = 1.4426950408889634
NEG = -1e30
HEAD = 64
ROWS = 16
POS = 8192
CHUNK = 4096
WIDE = 64
VROWS = 144


def kernel(
    hid_h, gain_h, wq_h, wo_h, enc_h, len_h, out,
    hid, gain, wq, lens, kbuf, vbuf, vt, nrm, nra, wqa, prt, prs, qall, qw0, qw1, s0, s1,
    msg, cmb, rep, pick, att, wo,
    load, wq_s, wq_r, nr_s, nr_r, ps_s, ps_r, q_s, q_r, m_s, m_r, a_s, a_r, t_s, t_r, y_s, y_r, x_s, x_r, c_s, c_r,
):
    s, g = lax.axis_index("seq"), lax.axis_index("grp")
    x, yc, p, c = s // 8, s % 8, s // 2, s % 2
    y = yc // 2
    apart = p != g
    turned = {"seq": 2 * g + c, "grp": p}

    def send(src, dst, ssem, rsem, where):
        return pltpu.make_async_remote_copy(
            src_ref=src, dst_ref=dst, send_sem=ssem, recv_sem=rsem, device_id=where, device_id_type=MESH
        )

    loads = [
        pltpu.make_async_copy(a, b, load.at[i])
        for i, (a, b) in enumerate(
            [(hid_h, hid), (gain_h, gain), (wq_h, wq), (len_h, lens), (enc_h.at[1], vbuf), (enc_h.at[0], kbuf)]
        )
    ]
    for one in loads:
        one.start()
    barrier = pltpu.get_barrier_semaphore()
    for o in range(1, 32):
        pl.semaphore_signal(barrier, inc=1, device_id={"seq": (s + o) % 32}, device_id_type=MESH)
    for o in range(1, 16):
        pl.semaphore_signal(barrier, inc=1, device_id={"grp": (g + o) % 16}, device_id_type=MESH)

    @pl.when(apart)
    def _():
        pl.semaphore_signal(barrier, inc=1, device_id=turned, device_id_type=MESH)

    loads[0].wait()
    loads[1].wait()
    loads[2].wait()
    wide = hid[...].astype(F32)
    scale = lax.rsqrt(jnp.mean(wide * wide, axis=-1, keepdims=True) + 1e-06)
    normed = (wide * scale * gain[...]).astype(BF16)
    for i in range(8):
        nrm[i] = jnp.concatenate([normed[:, j * 1024 + i * 128 : j * 1024 + i * 128 + 128] for j in range(4)], axis=1)
    nra[yc] = nrm[yc]
    wqa[x] = wq[...]

    pl.semaphore_wait(barrier, 46 + apart.astype(jnp.int32))

    gathers, sends = [], []
    for o in range(1, 8):
        to, other = (yc + o) % 8, (yc + 8 - o) % 8
        sends.append(send(nrm.at[to], nra.at[yc], nr_s.at[o], nr_r.at[yc], {"seq": x * 8 + to}))
        gathers.append(send(nrm.at[to], nra.at[other], nr_s.at[o], nr_r.at[other], {"seq": x * 8 + to}))
    for o in range(1, 4):
        to, other = (x + o) % 4, (x + 4 - o) % 4
        sends.append(send(wq, wqa.at[x], wq_s.at[o], wq_r.at[x], {"seq": to * 8 + yc}))
        gathers.append(send(wq, wqa.at[other], wq_s.at[o], wq_r.at[other], {"seq": to * 8 + yc}))
    for one in sends:
        one.start()

    turn = send(wo_h, wo.at[c, g], t_s, t_r, turned)
    stay = pltpu.make_async_copy(wo_h, wo.at[c, g], t_s)

    @pl.when(apart)
    def _():
        turn.start()

    @pl.when(jnp.logical_not(apart))
    def _():
        stay.start()

    loads[4].wait()
    for i in range(8):
        vt[0:128, i * 1024 : (i + 1) * 1024] = vbuf[i * 1024 : (i + 1) * 1024, :].T
    vt[128:VROWS, :] = jnp.ones((VROWS - 128, POS), BF16)
    row = lax.broadcasted_iota(jnp.int32, (64, 4096), 0)
    col = lax.broadcasted_iota(jnp.int32, (64, 4096), 1)
    rep[...] = ((row % 32 == col // 128) & (row // 32 == (col % 128) // HEAD)).astype(F32).astype(BF16)
    row = lax.broadcasted_iota(jnp.int32, (64, 512), 0)
    col = lax.broadcasted_iota(jnp.int32, (64, 512), 1)
    pick[...] = ((row % 32 == col // 16) & (col % 16 < 6) & (col % 2 == row // 32)).astype(F32).astype(BF16)
    loads[3].wait()

    for one in gathers:
        one.wait_recv()
    part = jnp.dot(nra[...].reshape(128, 512), wqa[...].reshape(512, 128), preferred_element_type=F32)
    prt[...] = part.reshape(8, ROWS, 128)
    prs[yc] = prt[yc]
    gathers = []
    for o in range(1, 8):
        to, other = (yc + o) % 8, (yc + 8 - o) % 8
        one = send(prt.at[to], prs.at[yc], ps_s.at[o], ps_r.at[yc], {"seq": x * 8 + to})
        one.start()
        sends.append(one)
        gathers.append(send(prt.at[to], prs.at[other], ps_s.at[o], ps_r.at[other], {"seq": x * 8 + to}))
    for one in gathers:
        one.wait_recv()
    total = prs[0]
    for i in range(1, 8):
        total = total + prs[i]
    qall[s] = total.astype(BF16)

    def plane(k):
        return (x + k) % 4

    for k in (0, 3, 2, 1):
        for o in range(1 if k == 0 else 0, 8):
            to = plane(k) * 8 + (yc + o) % 8
            one = send(qall.at[s], qall.at[s], q_s.at[k * 8 + o], q_r.at[s], {"seq": to})
            one.start()
            sends.append(one)

    lane = lax.broadcasted_iota(jnp.int32, (128, 128), 1)
    qws, sbufs = (qw0, qw1), (s0, s1)

    def take_queries(k):
        for o in range(1 if k == 0 else 0, 8):
            at = plane(k) * 8 + (yc + o) % 8
            send(qall.at[s], qall.at[at], q_s.at[0], q_r.at[at], {"seq": (s + 1) % 32}).wait_recv()
        q = qall[pl.ds(plane(k) * 8, 8)].reshape(128, 128).astype(F32) * LOG2E
        high = q.astype(BF16).astype(F32)
        low = q - high
        qw = qws[k % 2]
        for h in range(2):
            keep = (lane < HEAD) if h == 0 else (lane >= HEAD)
            qw[h * 128 : (h + 1) * 128, 0:128] = jnp.where(keep, high, 0.0).astype(BF16)
            qw[h * 128 : (h + 1) * 128, 128:256] = jnp.where(keep, low, 0.0).astype(BF16)

    def scores(k, i, top):
        keys = kbuf[pl.ds(i * CHUNK, CHUNK), :]
        keys = jnp.concatenate([keys, keys], axis=1)
        score = lax.dot_general(keys, qws[k % 2][...], NT, preferred_element_type=F32)
        left = lens[pl.ds(plane(k), 1), :] - s * POS - i * CHUNK
        ok = lax.broadcasted_iota(jnp.int32, (CHUNK, 128), 0) < left
        score = jnp.concatenate(
            [jnp.where(ok, score[:, :128], NEG), jnp.where(ok, score[:, 128:], NEG)], axis=1
        )
        sbufs[k % 2][pl.ds(i * CHUNK, CHUNK), :] = score
        return jnp.maximum(top, score.reshape(CHUNK // WIDE, WIDE, 256).max(axis=0))

    def weigh(k, i, peak, acc):
        weights = jnp.exp2(sbufs[k % 2][pl.ds(i * CHUNK, CHUNK), :] - peak).astype(BF16)
        values = vt[:, pl.ds(pl.multiple_of(i * CHUNK, CHUNK), CHUNK)]
        return acc + jnp.dot(values, weights, preferred_element_type=F32)

    def deliver(k, peak, acc):
        total = acc[128:129, :]
        scale = 1.0 / total
        both = jnp.concatenate(
            [acc[0:64, 0:128] * scale[:, 0:128], acc[64:128, 128:256] * scale[:, 128:256]], axis=0
        )
        msg[k, :, 0:ROWS, :] = both.T.astype(BF16).reshape(8, ROWS, 128)
        level = peak + jnp.log2(total)
        high = level.astype(BF16).astype(F32)
        mid = (level - high).astype(BF16).astype(F32)
        low = level - high - mid
        rows = [v[:, h * 128 : (h + 1) * 128] for v in (high, mid, low) for h in range(2)]
        rows = jnp.concatenate(rows + [jnp.zeros((10, 128), F32)], axis=0).astype(BF16)
        for o in range(8):
            msg[k, o, ROWS : 2 * ROWS, :] = rows
        if k == 0:
            cmb[s] = msg[0, yc]
        for o in range(1 if k == 0 else 0, 8):
            to = (yc + o) % 8
            one = send(msg.at[k, to], cmb.at[s], m_s.at[k * 8 + o], m_r.at[s], {"seq": plane(k) * 8 + to})
            one.start()
            sends.append(one)

    def background(stage):
        if stage == 0:
            pl.when(apart)(turn.wait_recv)
            pl.when(jnp.logical_not(apart))(stay.wait)
            for o in range(1, 4):
                to = x * 8 + ((y + o) % 4) * 2 + c
                one = send(wo.at[c, p], wo.at[c, p], y_s.at[o], y_r.at[y], {"seq": to})
                one.start()
                sends.append(one)
        if stage == 1:
            for o in range(1, 4):
                at = (y + o) % 4
                slot = wo.at[c, x * 4 + at]
                send(slot, slot, y_s.at[0], y_r.at[at], {"seq": (s + 1) % 32}).wait_recv()
            for o in range(1, 4):
                to = ((x + o) % 4) * 8 + yc
                four = wo.at[c, pl.ds(x * 4, 4)]
                one = send(four, four, x_s.at[o], x_r.at[x], {"seq": to})
                one.start()
                sends.append(one)
        if stage == 3:
            for o in range(1, 4):
                at = (x + o) % 4
                four = wo.at[c, pl.ds(at * 4, 4)]
                send(four, four, x_s.at[0], x_r.at[at], {"seq": (s + 1) % 32}).wait_recv()
            one = send(wo.at[c], wo.at[c], c_s, c_r, {"seq": s + 1 - 2 * c})
            one.start()
            sends.append(one)

    loads[5].wait()
    peak = None
    for stage in range(5):
        if stage < 4:
            take_queries(stage)

        def step(i, carry, stage=stage, peak=peak):
            top, acc = carry
            if stage < 4:
                top = scores(stage, i, top)
            if stage > 0:
                acc = weigh(stage - 1, i, peak, acc)
            return top, acc

        top, acc = lax.fori_loop(
            0, POS // CHUNK, step, (jnp.full((WIDE, 256), NEG, F32), jnp.zeros((VROWS, 256), F32))
        )
        if stage > 0:
            deliver(stage - 1, peak, acc)
        if stage < 4:
            peak = jnp.max(top, axis=0, keepdims=True)
        background(stage)

    for o in range(1, 32):
        at = (s + o) % 32
        send(cmb.at[at], cmb.at[at], m_s.at[0], m_r.at[at], {"seq": (s + 1) % 32}).wait_recv()
    level = jnp.dot(pick[...], cmb[:, ROWS : 2 * ROWS, :].reshape(512, 128), preferred_element_type=F32)
    shares = []
    for h in range(2):
        one = level[h * 32 : (h + 1) * 32]
        one = jnp.exp2(one - jnp.max(one, axis=0, keepdims=True))
        shares.append(one / jnp.sum(one, axis=0, keepdims=True))
    share = jnp.concatenate(shares, axis=0)
    high = share.astype(BF16)
    low = (share - high.astype(F32)).astype(BF16)
    own = (
        lax.broadcasted_iota(jnp.int32, (ROWS, 128), 1) == yc * ROWS + lax.broadcasted_iota(jnp.int32, (ROWS, 128), 0)
    ).astype(F32).astype(BF16)
    turned_share = lax.dot_general(own, high, NT, preferred_element_type=F32) + lax.dot_general(
        own, low, NT, preferred_element_type=F32
    )
    high = turned_share.astype(BF16)
    low = (turned_share - high.astype(F32)).astype(BF16)
    spread = jnp.dot(high, rep[...], preferred_element_type=F32) + jnp.dot(low, rep[...], preferred_element_type=F32)
    joined = jnp.zeros((ROWS, 128), F32)
    for i in range(32):
        joined = joined + spread[:, i * 128 : (i + 1) * 128] * cmb[i, 0:ROWS, :].astype(F32)
    att[g] = joined.astype(BF16)
    for o in range(1, 16):
        one = send(att.at[g], att.at[g], a_s.at[o], a_r.at[g], {"grp": (g + o) % 16})
        one.start()
        sends.append(one)
    send(wo.at[1 - c], wo.at[1 - c], c_s, c_r, {"seq": s + 1 - 2 * c}).wait_recv()
    for o in range(1, 16):
        at = (g + o) % 16
        send(att.at[at], att.at[at], a_s.at[0], a_r.at[at], {"grp": (g + 1) % 16}).wait_recv()
    attended = jnp.concatenate([att[i] for i in range(16)], axis=1)
    for h in range(2):
        mixed = jnp.dot(attended, wo[h].reshape(2048, 128), preferred_element_type=F32)
        base = hid[:, pl.ds(pl.multiple_of(g * 256 + h * 128, 128), 128)].astype(F32)
        out[:, h * 128 : (h + 1) * 128] = (base + mixed).astype(BF16)

    for one in sends:
        one.wait_send()
    pl.when(apart)(turn.wait_send)


def body(hidden, norm_gain, w_query, w_out, enc_cache, lengths):
    dma = pltpu.SemaphoreType.DMA
    vm = pltpu.VMEM
    any_space = pl.BlockSpec(memory_space=pl.ANY)
    return pl.pallas_call(
        kernel,
        out_shape=jax.ShapeDtypeStruct((ROWS, 256), BF16),
        in_specs=[any_space] * 6,
        out_specs=pl.BlockSpec(memory_space=pltpu.VMEM),
        scratch_shapes=[
            vm((ROWS, 4096), BF16), vm((1, 4096), F32), vm((128, 128), BF16), vm((4, 128), jnp.int32),
            vm((POS, 128), BF16), vm((POS, 128), BF16), vm((VROWS, POS), BF16),
            vm((8, ROWS, 512), BF16), vm((8, ROWS, 512), BF16), vm((4, 128, 128), BF16),
            vm((8, ROWS, 128), F32), vm((8, ROWS, 128), F32), vm((32, ROWS, 128), BF16),
            vm((256, 256), BF16), vm((256, 256), BF16), vm((POS, 256), F32), vm((POS, 256), F32),
            vm((4, 8, 2 * ROWS, 128), BF16), vm((32, 2 * ROWS, 128), BF16), vm((64, 4096), BF16), vm((64, 512), BF16),
            vm((16, ROWS, 128), BF16), vm((2, 16, 128, 128), BF16),
            dma((6,)), dma((4,)), dma((4,)), dma((8,)), dma((8,)), dma((8,)), dma((8,)), dma((32,)), dma((32,)),
            dma((32,)), dma((32,)), dma((16,)), dma((16,)), dma, dma, dma((4,)), dma((4,)), dma((4,)), dma((4,)), dma, dma,
        ],
        compiler_params=pltpu.CompilerParams(
            collective_id=0, has_side_effects=True, vmem_limit_bytes=56 * 2**20
        ),
        cost_estimate=pl.CostEstimate(flops=2200000000, bytes_accessed=6000000, transcendentals=8400000),
    )(hidden, norm_gain.reshape(1, 4096), w_query, w_out, enc_cache, lengths.reshape(4, 128))


def solution(mesh):
    placed = (P("seq", None), P(), P("seq", "grp"), P("grp", "seq"), P(None, "seq", "grp"), P())
    return jax.shard_map(body, mesh=mesh, in_specs=placed, out_specs=P("seq", "grp"), check_vma=False)
```

time: 564 us -> 62.4 us (0.11)
  the two profiles are of different devices: /device:TPU:1 before, /device:TPU:6 now
where the time goes in v1:
time: 62.4 us; the launch traced here: 62.3 us
  Pallas kernels  61 us (98%)
  local copies, waits for them, and re-layouts  1.3 us (2%)
    pallas_call x1, Pallas kernels, body(): pl.pallas_call(kernel, out_shape=jax.ShapeDtypeStruct((ROWS, 256), BF16),...  61 us
    unnamed x1, local copies, waits for them, and re-layouts  1.3 us

profile of v1, /device:TPU:6, one launch (start us, length us, event | category | flops | bytes accessed | tf_op | source)
XLA Modules:
  0.0 62.3 jit_solution(13224578830907669070)
XLA Ops:
  0.0 61.0 %shard_map.64 = bf16[16,256]{1,0:T(8,128)(2,1)} custom-call(bf16[16,4096]{1,0:T(8,128)(2,1)} %hid_h.1, f32[1,4096]{1,0:T(1,128)} %bitcast.2, bf16[128,128]{1,0:T(8,128)(2,1)} %wq_h.1, bf16[128,128]{1,0:T(8,128)(2,1)} %wo_h.1, bf16[2,8192,128]{2,1,0:T(8,128)(2,1)} %enc_h.1, s32[4,128]{1,0:T(4,128)} %bitcast.3), custom_call_target="tpu_custom_call" | custom-call | flops 2200000000 | bytes 6000000 | tf_op jit(solution)/shard_map/pallas_call | solution.py:290
  61.0 1.3 %copy.8 = bf16[16,256]{1,0:T(8,128)(2,1)} copy(bf16[16,256]{1,0:T(8,128)(2,1)} %shard_map.64) | data formatting | bytes 16384

commit v2 on v1

--- a/solution.py
+++ b/solution.py
@@ -21,15 +21,18 @@
 
 def kernel(
     hid_h, gain_h, wq_h, wo_h, enc_h, len_h, out,
-    hid, gain, wq, lens, kbuf, vbuf, vt, nrm, nra, wqa, prt, prs, qall, qw0, qw1, s0, s1,
+    hid, gain, wq, lens_in, lens, kbuf, vbuf, vt, nrm, nra, wqa, prt, prs, qall, qw0, qw1, s0, s1,
     msg, cmb, rep, pick, att, wo,
-    load, wq_s, wq_r, nr_s, nr_r, ps_s, ps_r, q_s, q_r, m_s, m_r, a_s, a_r, t_s, t_r, y_s, y_r, x_s, x_r, c_s, c_r,
+    load, wq_s, wq_r, nr_s, nr_r, ps_s, ps_r, q_s, q_r, m_s, m_r, a_s, a_r, t_s, t_r, w_s, w_r, c_s, c_r,
 ):
     s, g = lax.axis_index("seq"), lax.axis_index("grp")
-    x, yc, p, c = s // 8, s % 8, s // 2, s % 2
-    y = yc // 2
+    x, y, p, c = s // 8, (s // 2) % 4, s // 2, s % 2
+    e = x * 2 + c
     apart = p != g
     turned = {"seq": 2 * g + c, "grp": p}
+
+    def at_y(place, row):
+        return (place // 2) * 8 + row * 2 + place % 2
 
     def send(src, dst, ssem, rsem, where):
         return pltpu.make_async_remote_copy(
@@ -39,7 +42,7 @@
     loads = [
         pltpu.make_async_copy(a, b, load.at[i])
         for i, (a, b) in enumerate(
-            [(hid_h, hid), (gain_h, gain), (wq_h, wq), (len_h, lens), (enc_h.at[1], vbuf), (enc_h.at[0], kbuf)]
+            [(hid_h, hid), (gain_h, gain), (wq_h, wq), (len_h, lens_in), (enc_h.at[1], vbuf), (enc_h.at[0], kbuf)]
         )
     ]
     for one in loads:
@@ -61,21 +64,21 @@
     scale = lax.rsqrt(jnp.mean(wide * wide, axis=-1, keepdims=True) + 1e-06)
     normed = (wide * scale * gain[...]).astype(BF16)
     for i in range(8):
-        nrm[i] = jnp.concatenate([normed[:, j * 1024 + i * 128 : j * 1024 + i * 128 + 128] for j in range(4)], axis=1)
-    nra[yc] = nrm[yc]
-    wqa[x] = wq[...]
+        nrm[i] = jnp.concatenate([normed[:, at_y(i, j) * 128 : at_y(i, j) * 128 + 128] for j in range(4)], axis=1)
+    nra[e] = nrm[e]
+    wqa[y] = wq[...]
 
     pl.semaphore_wait(barrier, 46 + apart.astype(jnp.int32))
 
     gathers, sends = [], []
+    for o in range(1, 4):
+        to, other = (y + o) % 4, (y + 4 - o) % 4
+        sends.append(send(wq, wqa.at[y], wq_s.at[o], wq_r.at[y], {"seq": at_y(e, to)}))
+        gathers.append(send(wq, wqa.at[other], wq_s.at[o], wq_r.at[other], {"seq": at_y(e, to)}))
     for o in range(1, 8):
-        to, other = (yc + o) % 8, (yc + 8 - o) % 8
-        sends.append(send(nrm.at[to], nra.at[yc], nr_s.at[o], nr_r.at[yc], {"seq": x * 8 + to}))
-        gathers.append(send(nrm.at[to], nra.at[other], nr_s.at[o], nr_r.at[other], {"seq": x * 8 + to}))
-    for o in range(1, 4):
-        to, other = (x + o) % 4, (x + 4 - o) % 4
-        sends.append(send(wq, wqa.at[x], wq_s.at[o], wq_r.at[x], {"seq": to * 8 + yc}))
-        gathers.append(send(wq, wqa.at[other], wq_s.at[o], wq_r.at[other], {"seq": to * 8 + yc}))
+        to, other = (e + o) % 8, (e + 8 - o) % 8
+        sends.append(send(nrm.at[to], nra.at[e], nr_s.at[o], nr_r.at[e], {"seq": at_y(to, y)}))
+        gathers.append(send(nrm.at[to], nra.at[other], nr_s.at[o], nr_r.at[other], {"seq": at_y(to, y)}))
     for one in sends:
         one.start()
 
@@ -101,44 +104,56 @@
     col = lax.broadcasted_iota(jnp.int32, (64, 512), 1)
     pick[...] = ((row % 32 == col // 16) & (col % 16 < 6) & (col % 2 == row // 32)).astype(F32).astype(BF16)
     loads[3].wait()
+    for i in range(4):
+        lens[i : i + 1, :] = jnp.concatenate([lens_in[j : j + 1, i * 32 : i * 32 + 32] for j in range(4)], axis=1)
 
     for one in gathers:
         one.wait_recv()
     part = jnp.dot(nra[...].reshape(128, 512), wqa[...].reshape(512, 128), preferred_element_type=F32)
     prt[...] = part.reshape(8, ROWS, 128)
-    prs[yc] = prt[yc]
+    prs[e] = prt[e]
     gathers = []
     for o in range(1, 8):
-        to, other = (yc + o) % 8, (yc + 8 - o) % 8
-        one = send(prt.at[to], prs.at[yc], ps_s.at[o], ps_r.at[yc], {"seq": x * 8 + to})
+        to, other = (e + o) % 8, (e + 8 - o) % 8
+        one = send(prt.at[to], prs.at[e], ps_s.at[o], ps_r.at[e], {"seq": at_y(to, y)})
         one.start()
         sends.append(one)
-        gathers.append(send(prt.at[to], prs.at[other], ps_s.at[o], ps_r.at[other], {"seq": x * 8 + to}))
+        gathers.append(send(prt.at[to], prs.at[other], ps_s.at[o], ps_r.at[other], {"seq": at_y(to, y)}))
     for one in gathers:
         one.wait_recv()
     total = prs[0]
     for i in range(1, 8):
         total = total + prs[i]
-    qall[s] = total.astype(BF16)
-
-    def plane(k):
-        return (x + k) % 4
-
-    for k in (0, 3, 2, 1):
+    me = y * 8 + e
+    qall[me] = total.astype(BF16)
+    order = (0, 2, 3, 1)
+
+    def group(k):
+        return y ^ order[k]
+
+    for k in range(4):
         for o in range(1 if k == 0 else 0, 8):
-            to = plane(k) * 8 + (yc + o) % 8
-            one = send(qall.at[s], qall.at[s], q_s.at[k * 8 + o], q_r.at[s], {"seq": to})
+            one = send(
+                qall.at[me], qall.at[me], q_s.at[k * 8 + o], q_r.at[me], {"seq": at_y((e + o) % 8, group(k))}
+            )
             one.start()
             sends.append(one)
 
+    pl.when(apart)(turn.wait_recv)
+    pl.when(jnp.logical_not(apart))(stay.wait)
+    for o in range(1, 16):
+        one = send(wo.at[c, p], wo.at[c, p], w_s.at[o], w_r.at[p], {"seq": 2 * ((p + o) % 16) + c})
+        one.start()
+        sends.append(one)
+
     lane = lax.broadcasted_iota(jnp.int32, (128, 128), 1)
     qws, sbufs = (qw0, qw1), (s0, s1)
 
     def take_queries(k):
         for o in range(1 if k == 0 else 0, 8):
-            at = plane(k) * 8 + (yc + o) % 8
+            at = group(k) * 8 + (e + o) % 8
             send(qall.at[s], qall.at[at], q_s.at[0], q_r.at[at], {"seq": (s + 1) % 32}).wait_recv()
-        q = qall[pl.ds(plane(k) * 8, 8)].reshape(128, 128).astype(F32) * LOG2E
+        q = qall[pl.ds(group(k) * 8, 8)].reshape(128, 128).astype(F32) * LOG2E
         high = q.astype(BF16).astype(F32)
         low = q - high
         qw = qws[k % 2]
@@ -151,7 +166,7 @@
         keys = kbuf[pl.ds(i * CHUNK, CHUNK), :]
         keys = jnp.concatenate([keys, keys], axis=1)
         score = lax.dot_general(keys, qws[k % 2][...], NT, preferred_element_type=F32)
-        left = lens[pl.ds(plane(k), 1), :] - s * POS - i * CHUNK
+        left = lens[pl.ds(group(k), 1), :] - s * POS - i * CHUNK
         ok = lax.broadcasted_iota(jnp.int32, (CHUNK, 128), 0) < left
         score = jnp.concatenate(
             [jnp.where(ok, score[:, :128], NEG), jnp.where(ok, score[:, 128:], NEG)], axis=1
@@ -180,39 +195,10 @@
         for o in range(8):
             msg[k, o, ROWS : 2 * ROWS, :] = rows
         if k == 0:
-            cmb[s] = msg[0, yc]
+            cmb[s] = msg[0, e]
         for o in range(1 if k == 0 else 0, 8):
-            to = (yc + o) % 8
-            one = send(msg.at[k, to], cmb.at[s], m_s.at[k * 8 + o], m_r.at[s], {"seq": plane(k) * 8 + to})
-            one.start()
-            sends.append(one)
-
-    def background(stage):
-        if stage == 0:
-            pl.when(apart)(turn.wait_recv)
-            pl.when(jnp.logical_not(apart))(stay.wait)
-            for o in range(1, 4):
-                to = x * 8 + ((y + o) % 4) * 2 + c
-                one = send(wo.at[c, p], wo.at[c, p], y_s.at[o], y_r.at[y], {"seq": to})
-                one.start()
-                sends.append(one)
-        if stage == 1:
-            for o in range(1, 4):
-                at = (y + o) % 4
-                slot = wo.at[c, x * 4 + at]
-                send(slot, slot, y_s.at[0], y_r.at[at], {"seq": (s + 1) % 32}).wait_recv()
-            for o in range(1, 4):
-                to = ((x + o) % 4) * 8 + yc
-                four = wo.at[c, pl.ds(x * 4, 4)]
-                one = send(four, four, x_s.at[o], x_r.at[x], {"seq": to})
-                one.start()
-                sends.append(one)
-        if stage == 3:
-            for o in range(1, 4):
-                at = (x + o) % 4
-                four = wo.at[c, pl.ds(at * 4, 4)]
-                send(four, four, x_s.at[0], x_r.at[at], {"seq": (s + 1) % 32}).wait_recv()
-            one = send(wo.at[c], wo.at[c], c_s, c_r, {"seq": s + 1 - 2 * c})
+            to = (e + o) % 8
+            one = send(msg.at[k, to], cmb.at[s], m_s.at[k * 8 + o], m_r.at[s], {"seq": at_y(to, group(k))})
             one.start()
             sends.append(one)
 
@@ -237,7 +223,13 @@
             deliver(stage - 1, peak, acc)
         if stage < 4:
             peak = jnp.max(top, axis=0, keepdims=True)
-        background(stage)
+
+    for o in range(1, 16):
+        at = (p + o) % 16
+        send(wo.at[c, at], wo.at[c, at], w_s.at[0], w_r.at[at], {"seq": (s + 1) % 32}).wait_recv()
+    swap = send(wo.at[c], wo.at[c], c_s, c_r, {"seq": s + 1 - 2 * c})
+    swap.start()
+    sends.append(swap)
 
     for o in range(1, 32):
         at = (s + o) % 32
@@ -252,7 +244,7 @@
     high = share.astype(BF16)
     low = (share - high.astype(F32)).astype(BF16)
     own = (
-        lax.broadcasted_iota(jnp.int32, (ROWS, 128), 1) == yc * ROWS + lax.broadcasted_iota(jnp.int32, (ROWS, 128), 0)
+        lax.broadcasted_iota(jnp.int32, (ROWS, 128), 1) == e * ROWS + lax.broadcasted_iota(jnp.int32, (ROWS, 128), 0)
     ).astype(F32).astype(BF16)
     turned_share = lax.dot_general(own, high, NT, preferred_element_type=F32) + lax.dot_general(
         own, low, NT, preferred_element_type=F32
@@ -293,7 +285,7 @@
         in_specs=[any_space] * 6,
         out_specs=pl.BlockSpec(memory_space=pltpu.VMEM),
         scratch_shapes=[
-            vm((ROWS, 4096), BF16), vm((1, 4096), F32), vm((128, 128), BF16), vm((4, 128), jnp.int32),
+            vm((ROWS, 4096), BF16), vm((1, 4096), F32), vm((128, 128), BF16), vm((4, 128), jnp.int32), vm((4, 128), jnp.int32),
             vm((POS, 128), BF16), vm((POS, 128), BF16), vm((VROWS, POS), BF16),
             vm((8, ROWS, 512), BF16), vm((8, ROWS, 512), BF16), vm((4, 128, 128), BF16),
             vm((8, ROWS, 128), F32), vm((8, ROWS, 128), F32), vm((32, ROWS, 128), BF16),
@@ -301,7 +293,7 @@
             vm((4, 8, 2 * ROWS, 128), BF16), vm((32, 2 * ROWS, 128), BF16), vm((64, 4096), BF16), vm((64, 512), BF16),
             vm((16, ROWS, 128), BF16), vm((2, 16, 128, 128), BF16),
             dma((6,)), dma((4,)), dma((4,)), dma((8,)), dma((8,)), dma((8,)), dma((8,)), dma((32,)), dma((32,)),
-            dma((32,)), dma((32,)), dma((16,)), dma((16,)), dma, dma, dma((4,)), dma((4,)), dma((4,)), dma((4,)), dma, dma,
+            dma((32,)), dma((32,)), dma((16,)), dma((16,)), dma, dma, dma((16,)), dma((16,)), dma, dma,
         ],
         compiler_params=pltpu.CompilerParams(
             collective_id=0, has_side_effects=True, vmem_limit_bytes=56 * 2**20

time: 62.4 us -> 58.4 us (0.936)
  the two profiles are of different devices: /device:TPU:6 before, /device:TPU:1 now
where the time goes in v2:
time: 58.4 us; the launch traced here: 58.2 us
  Pallas kernels  56.9 us (97%)
  local copies, waits for them, and re-layouts  1.3 us (2%)
    pallas_call x1, Pallas kernels, body(): pl.pallas_call(kernel, out_shape=jax.ShapeDtypeStruct((ROWS, 256), BF16),...  56.9 us
    unnamed x1, local copies, waits for them, and re-layouts  1.3 us

profile of v2, /device:TPU:1, one launch (start us, length us, event | category | flops | bytes accessed | tf_op | source)
XLA Modules:
  0.0 58.2 jit_solution(9356669569018234233)
XLA Ops:
  0.0 56.9 %shard_map.64 = bf16[16,256]{1,0:T(8,128)(2,1)} custom-call(bf16[16,4096]{1,0:T(8,128)(2,1)} %hid_h.1, f32[1,4096]{1,0:T(1,128)} %bitcast.2, bf16[128,128]{1,0:T(8,128)(2,1)} %wq_h.1, bf16[128,128]{1,0:T(8,128)(2,1)} %wo_h.1, bf16[2,8192,128]{2,1,0:T(8,128)(2,1)} %enc_h.1, s32[4,128]{1,0:T(4,128)} %bitcast.3), custom_call_target="tpu_custom_call" | custom-call | flops 2200000000 | bytes 6000000 | tf_op jit(solution)/shard_map/pallas_call | solution.py:282
  56.9 1.3 %copy.8 = bf16[16,256]{1,0:T(8,128)(2,1)} copy(bf16[16,256]{1,0:T(8,128)(2,1)} %shard_map.64) | data formatting | bytes 16384

commit v3 on v2

--- a/solution.py
+++ b/solution.py
@@ -48,8 +48,10 @@
     for one in loads:
         one.start()
     barrier = pltpu.get_barrier_semaphore()
-    for o in range(1, 32):
-        pl.semaphore_signal(barrier, inc=1, device_id={"seq": (s + o) % 32}, device_id_type=MESH)
+    for o in range(1, 8):
+        pl.semaphore_signal(barrier, inc=1, device_id={"seq": at_y((e + o) % 8, y)}, device_id_type=MESH)
+    for o in range(1, 4):
+        pl.semaphore_signal(barrier, inc=1, device_id={"seq": at_y(e, (y + o) % 4)}, device_id_type=MESH)
     for o in range(1, 16):
         pl.semaphore_signal(barrier, inc=1, device_id={"grp": (g + o) % 16}, device_id_type=MESH)
 
@@ -68,7 +70,7 @@
     nra[e] = nrm[e]
     wqa[y] = wq[...]
 
-    pl.semaphore_wait(barrier, 46 + apart.astype(jnp.int32))
+    pl.semaphore_wait(barrier, 25 + apart.astype(jnp.int32))
 
     gathers, sends = [], []
     for o in range(1, 4):
@@ -81,17 +83,6 @@
         gathers.append(send(nrm.at[to], nra.at[other], nr_s.at[o], nr_r.at[other], {"seq": at_y(to, y)}))
     for one in sends:
         one.start()
-
-    turn = send(wo_h, wo.at[c, g], t_s, t_r, turned)
-    stay = pltpu.make_async_copy(wo_h, wo.at[c, g], t_s)
-
-    @pl.when(apart)
-    def _():
-        turn.start()
-
-    @pl.when(jnp.logical_not(apart))
-    def _():
-        stay.start()
 
     loads[4].wait()
     for i in range(8):
@@ -119,6 +110,17 @@
         one.start()
         sends.append(one)
         gathers.append(send(prt.at[to], prs.at[other], ps_s.at[o], ps_r.at[other], {"seq": at_y(to, y)}))
+    turn = send(wo_h, wo.at[c, g], t_s, t_r, turned)
+    stay = pltpu.make_async_copy(wo_h, wo.at[c, g], t_s)
+
+    @pl.when(apart)
+    def _():
+        turn.start()
+
+    @pl.when(jnp.logical_not(apart))
+    def _():
+        stay.start()
+
     for one in gathers:
         one.wait_recv()
     total = prs[0]
@@ -139,12 +141,13 @@
             one.start()
             sends.append(one)
 
-    pl.when(apart)(turn.wait_recv)
-    pl.when(jnp.logical_not(apart))(stay.wait)
-    for o in range(1, 16):
-        one = send(wo.at[c, p], wo.at[c, p], w_s.at[o], w_r.at[p], {"seq": 2 * ((p + o) % 16) + c})
-        one.start()
-        sends.append(one)
+    def spread_columns():
+        pl.when(apart)(turn.wait_recv)
+        pl.when(jnp.logical_not(apart))(stay.wait)
+        for o in range(1, 16):
+            one = send(wo.at[c, p], wo.at[c, p], w_s.at[o], w_r.at[p], {"seq": 2 * ((p + o) % 16) + c})
+            one.start()
+            sends.append(one)
 
     lane = lax.broadcasted_iota(jnp.int32, (128, 128), 1)
     qws, sbufs = (qw0, qw1), (s0, s1)
@@ -207,6 +210,8 @@
     for stage in range(5):
         if stage < 4:
             take_queries(stage)
+        if stage == 1:
+            spread_columns()
 
         def step(i, carry, stage=stage, peak=peak):
             top, acc = carry

time: 58.4 us -> 60.6 us (1.038)
  Pallas kernels: 56.9 us -> 59.1 us
    pallas_call x1, Pallas kernels: 56.9 us -> 59.1 us  [body(): pl.pallas_call(kernel, out_shape=jax.ShapeDtypeStruct((ROWS, 256), BF16),...]
where the time goes in v3:
time: 60.6 us; the launch traced here: 60.5 us
  Pallas kernels  59.1 us (98%)
  local copies, waits for them, and re-layouts  1.3 us (2%)
    pallas_call x1, Pallas kernels, body(): pl.pallas_call(kernel, out_shape=jax.ShapeDtypeStruct((ROWS, 256), BF16),...  59.1 us
    unnamed x1, local copies, waits for them, and re-layouts  1.3 us

profile of v3, /device:TPU:1, one launch (start us, length us, event | category | flops | bytes accessed | tf_op | source)
XLA Modules:
  0.0 60.5 jit_solution(2854138092869758065)
XLA Ops:
  0.0 59.1 %shard_map.64 = bf16[16,256]{1,0:T(8,128)(2,1)} custom-call(bf16[16,4096]{1,0:T(8,128)(2,1)} %hid_h.1, f32[1,4096]{1,0:T(1,128)} %bitcast.2, bf16[128,128]{1,0:T(8,128)(2,1)} %wq_h.1, bf16[128,128]{1,0:T(8,128)(2,1)} %wo_h.1, bf16[2,8192,128]{2,1,0:T(8,128)(2,1)} %enc_h.1, s32[4,128]{1,0:T(4,128)} %bitcast.3), custom_call_target="tpu_custom_call" | custom-call | flops 2200000000 | bytes 6000000 | tf_op jit(solution)/shard_map/pallas_call | solution.py:287
  59.2 1.3 %copy.8 = bf16[16,256]{1,0:T(8,128)(2,1)} copy(bf16[16,256]{1,0:T(8,128)(2,1)} %shard_map.64) | data formatting | bytes 16384

commit v4 on v2

--- a/solution.py
+++ b/solution.py
@@ -11,6 +11,7 @@
 NT = (((1,), (1,)), ((), ()))
 LOG2E = 1.4426950408889634
 NEG = -1e30
+FOURTH = 2
 HEAD = 64
 ROWS = 16
 POS = 8192
@@ -48,8 +49,10 @@
     for one in loads:
         one.start()
     barrier = pltpu.get_barrier_semaphore()
-    for o in range(1, 32):
-        pl.semaphore_signal(barrier, inc=1, device_id={"seq": (s + o) % 32}, device_id_type=MESH)
+    for o in range(1, 8):
+        pl.semaphore_signal(barrier, inc=1, device_id={"seq": at_y((e + o) % 8, y)}, device_id_type=MESH)
+    for o in range(1, 4):
+        pl.semaphore_signal(barrier, inc=1, device_id={"seq": at_y(e, (y + o) % 4)}, device_id_type=MESH)
     for o in range(1, 16):
         pl.semaphore_signal(barrier, inc=1, device_id={"grp": (g + o) % 16}, device_id_type=MESH)
 
@@ -68,7 +71,7 @@
     nra[e] = nrm[e]
     wqa[y] = wq[...]
 
-    pl.semaphore_wait(barrier, 46 + apart.astype(jnp.int32))
+    pl.semaphore_wait(barrier, 25 + apart.astype(jnp.int32))
 
     gathers, sends = [], []
     for o in range(1, 4):
@@ -106,6 +109,25 @@
     loads[3].wait()
     for i in range(4):
         lens[i : i + 1, :] = jnp.concatenate([lens_in[j : j + 1, i * 32 : i * 32 + 32] for j in range(4)], axis=1)
+
+    def spread_columns(part):
+        if part == 0:
+            pl.when(apart)(turn.wait_recv)
+            pl.when(jnp.logical_not(apart))(stay.wait)
+            for o in (2, 1, 3):
+                one = send(wo.at[c, p], wo.at[c, p], w_s.at[o], w_r.at[y], {"seq": at_y(e, (y + o) % 4)})
+                one.start()
+                sends.append(one)
+        if part == FOURTH:
+            for o in range(1, 4):
+                at = (y + o) % 4
+                slot = wo.at[c, x * 4 + at]
+                send(slot, slot, w_s.at[0], w_r.at[at], {"seq": (s + 1) % 32}).wait_recv()
+            four = wo.at[c, pl.ds(x * 4, 4)]
+            for o in (2, 1, 3):
+                one = send(four, four, w_s.at[4 + o], w_r.at[4 + x], {"seq": ((x + o) % 4) * 8 + y * 2 + c})
+                one.start()
+                sends.append(one)
 
     for one in gathers:
         one.wait_recv()
@@ -128,23 +150,18 @@
     qall[me] = total.astype(BF16)
     order = (0, 2, 3, 1)
 
+    far_first = (4, 5, 3, 6, 2, 7, 1, 0)
+
     def group(k):
         return y ^ order[k]
 
     for k in range(4):
-        for o in range(1 if k == 0 else 0, 8):
+        for o in far_first[: 7 if k == 0 else 8]:
             one = send(
                 qall.at[me], qall.at[me], q_s.at[k * 8 + o], q_r.at[me], {"seq": at_y((e + o) % 8, group(k))}
             )
             one.start()
             sends.append(one)
-
-    pl.when(apart)(turn.wait_recv)
-    pl.when(jnp.logical_not(apart))(stay.wait)
-    for o in range(1, 16):
-        one = send(wo.at[c, p], wo.at[c, p], w_s.at[o], w_r.at[p], {"seq": 2 * ((p + o) % 16) + c})
-        one.start()
-        sends.append(one)
 
     lane = lax.broadcasted_iota(jnp.int32, (128, 128), 1)
     qws, sbufs = (qw0, qw1), (s0, s1)
@@ -196,7 +213,7 @@
             msg[k, o, ROWS : 2 * ROWS, :] = rows
         if k == 0:
             cmb[s] = msg[0, e]
-        for o in range(1 if k == 0 else 0, 8):
+        for o in far_first[: 7 if k == 0 else 8]:
             to = (e + o) % 8
             one = send(msg.at[k, to], cmb.at[s], m_s.at[k * 8 + o], m_r.at[s], {"seq": at_y(to, group(k))})
             one.start()
@@ -207,6 +224,8 @@
     for stage in range(5):
         if stage < 4:
             take_queries(stage)
+            if stage < 3:
+                spread_columns(stage)
 
         def step(i, carry, stage=stage, peak=peak):
             top, acc = carry
@@ -224,9 +243,10 @@
         if stage < 4:
             peak = jnp.max(top, axis=0, keepdims=True)
 
-    for o in range(1, 16):
-        at = (p + o) % 16
-        send(wo.at[c, at], wo.at[c, at], w_s.at[0], w_r.at[at], {"seq": (s + 1) % 32}).wait_recv()
+    for o in range(1, 4):
+        at = (x + o) % 4
+        four = wo.at[c, pl.ds(at * 4, 4)]
+        send(four, four, w_s.at[0], w_r.at[4 + at], {"seq": (s + 1) % 32}).wait_recv()
     swap = send(wo.at[c], wo.at[c], c_s, c_r, {"seq": s + 1 - 2 * c})
     swap.start()
     sends.append(swap)
@@ -256,7 +276,7 @@
     for i in range(32):
         joined = joined + spread[:, i * 128 : (i + 1) * 128] * cmb[i, 0:ROWS, :].astype(F32)
     att[g] = joined.astype(BF16)
-    for o in range(1, 16):
+    for o in (9, 7, 8, 11, 5, 10, 6, 13, 3, 12, 4, 15, 1, 14, 2):
         one = send(att.at[g], att.at[g], a_s.at[o], a_r.at[g], {"grp": (g + o) % 16})
         one.start()
         sends.append(one)

time: 58.4 us -> 56.3 us (0.964)
  Pallas kernels: 56.9 us -> 54.8 us
    pallas_call x1, Pallas kernels: 56.9 us -> 54.8 us  [body(): pl.pallas_call(kernel, out_shape=jax.ShapeDtypeStruct((ROWS, 256), BF16),...]
where the time goes in v4:
time: 56.3 us; the launch traced here: 56.1 us
  Pallas kernels  54.8 us (97%)
  local copies, waits for them, and re-layouts  1.3 us (2%)
    pallas_call x1, Pallas kernels, body(): pl.pallas_call(kernel, out_shape=jax.ShapeDtypeStruct((ROWS, 256), BF16),...  54.8 us
    unnamed x1, local copies, waits for them, and re-layouts  1.3 us

profile of v4, /device:TPU:1, one launch (start us, length us, event | category | flops | bytes accessed | tf_op | source)
XLA Modules:
  0.0 56.1 jit_solution(12357999335021984225)
XLA Ops:
  0.0 54.8 %shard_map.64 = bf16[16,256]{1,0:T(8,128)(2,1)} custom-call(bf16[16,4096]{1,0:T(8,128)(2,1)} %hid_h.1, f32[1,4096]{1,0:T(1,128)} %bitcast.2, bf16[128,128]{1,0:T(8,128)(2,1)} %wq_h.1, bf16[128,128]{1,0:T(8,128)(2,1)} %wo_h.1, bf16[2,8192,128]{2,1,0:T(8,128)(2,1)} %enc_h.1, s32[4,128]{1,0:T(4,128)} %bitcast.3), custom_call_target="tpu_custom_call" | custom-call | flops 2200000000 | bytes 6000000 | tf_op jit(solution)/shard_map/pallas_call | solution.py:302
  54.8 1.3 %copy.8 = bf16[16,256]{1,0:T(8,128)(2,1)} copy(bf16[16,256]{1,0:T(8,128)(2,1)} %shard_map.64) | data formatting | bytes 16384
